TPU v7x, 32 devices: a whole 2x2x4 slice. The times are simulated.
32 devices in a mesh: rows: 4 (over z), protos: 8 (over y, x, core).
Axes of the slice: x: 2, y: 2, z: 4, core: 2. Of those that a mesh axis runs over, the one named last changes fastest.
Arguments:
- teacher_rows: bfloat16 [4096, 256], P(('rows', 'protos')), may hold values from -16 to 16
- student_rows: bfloat16 [4096, 256], P(('rows', 'protos')), may hold values from -16 to 16
- prototypes: bfloat16 [256, 131072], P(None, 'protos'), may hold values from -16 to 16
Outputs:
- row_grads: float32 [4096, 256], P(('rows', 'protos'))
- row_loss: float32 [4096], P(('rows', 'protos'))
All inputs are finite; a program needn't handle non-finite values.
Results may differ from a plain program's by a relative error of at most 0.0015.
Values may be sent and summed in bfloat16 or wider, within the bound.
No kernel may reach another device: no remote copies, remote signals or barrier semaphores. Data moves between devices by JAX's collectives and lax.ppermute only.
A program may use at most 192 MiB of HBM per device.

v0:
```python
import jax
import jax.numpy as jnp
from jax import lax
from jax.sharding import PartitionSpec as P

ITERS = 3


EPSILON = 1e-06
TEACHER_TEMP = 0.04
STUDENT_TEMP = 0.1


def unit_rows(values):
    floats = values.astype(jnp.float32)
    norms = jnp.sqrt(jnp.sum(floats * floats, axis=1, keepdims=True) + EPSILON)
    return (floats / norms, norms)


def on_device(teacher_rows, student_rows, prototypes):
    teacher_all, student_all = (
        lax.all_gather(teacher_rows, "protos", axis=0, tiled=True),
        lax.all_gather(student_rows, "protos", axis=0, tiled=True),
    )
    proto_float = prototypes.astype(jnp.float32)
    proto_norm = jnp.sqrt(jnp.sum(proto_float * proto_float, axis=0, keepdims=True) + EPSILON)
    proto_unit = proto_float / proto_norm
    proto_half = proto_unit.astype(jnp.bfloat16)
    teacher_unit = unit_rows(teacher_all)[0]
    student_unit = unit_rows(student_all)[0].astype(jnp.bfloat16)
    teacher_exp = jnp.exp(
        jnp.dot(
            teacher_unit,
            proto_unit,
            precision=lax.Precision.HIGHEST,
            preferred_element_type=jnp.float32,
        )
        / TEACHER_TEMP
    )
    student_logit = (
        jnp.dot(student_unit, proto_half, preferred_element_type=jnp.float32) / STUDENT_TEMP
    )
    student_part = jnp.sum(jnp.exp(student_logit), axis=1)
    weights = jnp.ones((teacher_exp.shape[0],), jnp.float32)
    inverse = jnp.ones((teacher_exp.shape[1],), jnp.float32)
    for sweep in range(ITERS):
        col_part = jnp.sum(teacher_exp * weights[:, None], axis=0)
        inverse = 1.0 / lax.psum(col_part, "rows")
        row_part = jnp.sum(teacher_exp * inverse[None, :], axis=1)
        row_total = lax.psum(row_part, "protos")
        weights = 1.0 / row_total
    sample_total = lax.psum(student_part, "protos")
    targets = teacher_exp * inverse[None, :] * weights[:, None]
    signal = (jnp.exp(student_logit) / sample_total[:, None] - targets).astype(jnp.bfloat16)
    loss_part = jnp.sum(targets * student_logit, axis=1)
    rows_own = student_rows.shape[0]
    offset = lax.axis_index("protos") * rows_own
    cross = lax.psum_scatter(loss_part, "protos", scatter_dimension=0, tiled=True)
    log_total = lax.dynamic_slice_in_dim(jnp.log(sample_total), offset, rows_own, 0)
    row_loss = log_total - cross
    direction = lax.psum_scatter(
        lax.dot_general(
            signal, proto_half, (((1,), (1,)), ((), ())), preferred_element_type=jnp.float32
        )
        / STUDENT_TEMP,
        "protos",
        scatter_dimension=0,
        tiled=True,
    )
    own_unit, own_norm = unit_rows(student_rows)
    radial = jnp.sum(own_unit * direction, axis=1, keepdims=True)
    row_grads = (direction - own_unit * radial) / own_norm
    return (row_grads, row_loss)


def solution(mesh):
    in_specs = (P(("rows", "protos"), None), P(("rows", "protos"), None), P(None, "protos"))
    out_specs = (P(("rows", "protos"), None), P(("rows", "protos")))
    return jax.shard_map(
        on_device, mesh=mesh, in_specs=in_specs, out_specs=out_specs, check_vma=False
    )
```

profile of v0, /device:TPU:0, one launch (start us, length us, event | category | flops | bytes accessed | tf_op | source)
XLA Modules:
  0.0 491.2 jit_solution(7603261303624061642)
XLA Ops:
  7.2 0.0 all-reduce.6.cloned.1.call-start
  7.2 11.6 %all_gather.7 = bf16[1024,256]{1,0:T(8,128)(2,1)S(1)} all-gather(bf16[128,256]{1,0:T(8,128)(2,1)} %param.3), channel_id=1, replica_groups=mesh['rows'=4,'protos'=8] {'protos'}, dimensions={0}, use_global_device_ids=true | all-gather | bytes 589824 | tf_op jit(solution)/shard_map/all_gather | solution.py:22
  18.8 0.2 fusion.7
  19.0 0.2 convert_divide_fusion.4.clone.5
  19.3 5.1 %fusion.1 = f32[16384]{0:T(1024)S(1)} fusion(bf16[256,16384]{1,0:T(8,128)(2,1)} %param.5), kind=kLoop, calls=%fused_computation.12 | loop fusion | flops 12566528 | bytes 8454144 | tf_op jit(solution)/shard_map/reduce_sum | solution.py:26
  24.4 0.0 copy-start
  24.4 65.2 %fusion.16 = (f32[16384]{0:T(1024)}, f32[1024,16384]{1,0:T(8,128)}) fusion(bf16[256,16384]{1,0:T(8,128)(2,1)} %param.5, f32[16384]{0:T(1024)S(1)} %add_sqrt_fusion, f32[1024,256]{1,0:T(8,128)S(1)} %convert_divide_fusion.4.clone.5), kind=kOutput, calls=%fused_computation.43 | convolution fusion | flops 51581534208 | bytes 76677120 | tf_op jit(solution)/shard_map/dot_general | solution.py:32
  89.6 0.0 all-reduce.6.cloned.1.call-update
  89.6 0.0 all-reduce.8.cloned.1.call-start
  89.7 0.0 copy-done
  89.7 9.7 %all_gather.6 = bf16[1024,256]{1,0:T(8,128)(2,1)S(1)} all-gather(bf16[128,256]{1,0:T(8,128)(2,1)S(1)} %copy-done), channel_id=1, replica_groups=mesh['rows'=4,'protos'=8] {'protos'}, dimensions={0}, use_global_device_ids=true | all-gather | bytes 589824 | tf_op jit(solution)/shard_map/all_gather | solution.py:23
  99.4 24.6 %all-reduce.6.cloned.1.call-done = f32[16384]{0:T(1024)} async-done(((f32[16384]{0:T(1024)}), f32[16384]{0:T(1024)}) %all-reduce.6.cloned.1.call-update) | async-done | bytes 65552 | tf_op jit(solution)/shard_map/psum | solution.py:48
  124.1 0.9 broadcast_divide_fusion.2
  124.9 20.9 %multiply_reduce_fusion.4 = f32[1024]{0:T(1024)S(1)} fusion(f32[1024,16384]{1,0:T(8,128)} %get-tuple-element.7, f32[16384]{0:T(1024)S(1)} %broadcast_divide_fusion.2), kind=kLoop, calls=%fused_computation.5 | loop fusion | flops 33553408 | bytes 67178496 | tf_op jit(solution)/shard_map/reduce_sum | solution.py:49
  145.8 11.8 %psum.51 = f32[1024]{0:T(1024)S(1)} all-reduce(f32[1024]{0:T(1024)S(1)} %multiply_reduce_fusion.4), channel_id=1, replica_groups=mesh['rows'=4,'protos'=8] {'protos'}, use_global_device_ids=true, to_apply=%region_8.0 | all-reduce | flops 1024 | bytes 8192 | tf_op jit(solution)/shard_map/psum | solution.py:50
  157.7 21.5 %multiply_reduce_fusion.3 = f32[16384]{0:T(1024)} fusion(f32[1024,16384]{1,0:T(8,128)} %get-tuple-element.7, f32[1024]{0:T(1024)S(1)} %broadcast_divide_fusion.5), kind=kLoop, calls=%fused_computation.4 | loop fusion | flops 33538048 | bytes 67178496 | tf_op jit(solution)/shard_map/reduce_sum | solution.py:47
  179.2 0.0 all-reduce.8.cloned.1.call-update
  179.2 0.0 all-reduce.10.cloned.1.call-start
  179.2 0.2 fusion.5
  179.4 32.7 %all-reduce.8.cloned.1.call-done = f32[16384]{0:T(1024)} async-done(((f32[16384]{0:T(1024)}), f32[16384]{0:T(1024)}) %all-reduce.8.cloned.1.call-update) | async-done | bytes 65552 | tf_op jit(solution)/shard_map/psum | solution.py:48
  212.1 0.9 broadcast_divide_fusion.1
  213.0 20.9 %multiply_reduce_fusion.2 = f32[1024]{0:T(1024)S(1)} fusion(f32[1024,16384]{1,0:T(8,128)} %get-tuple-element.7, f32[16384]{0:T(1024)S(1)} %broadcast_divide_fusion.1), kind=kLoop, calls=%fused_computation.3 | loop fusion | flops 33553408 | bytes 67178496 | tf_op jit(solution)/shard_map/reduce_sum | solution.py:49
  233.9 11.8 %psum.53 = f32[1024]{0:T(1024)S(1)} all-reduce(f32[1024]{0:T(1024)S(1)} %multiply_reduce_fusion.2), channel_id=1, replica_groups=mesh['rows'=4,'protos'=8] {'protos'}, use_global_device_ids=true, to_apply=%region_12.0 | all-reduce | flops 1024 | bytes 8192 | tf_op jit(solution)/shard_map/psum | solution.py:50
  245.7 21.5 %multiply_reduce_fusion.1 = f32[16384]{0:T(1024)} fusion(f32[1024,16384]{1,0:T(8,128)} %get-tuple-element.7, f32[1024]{0:T(1024)S(1)} %broadcast_divide_fusion.4), kind=kLoop, calls=%fused_computation.2 | loop fusion | flops 33538048 | bytes 67178496 | tf_op jit(solution)/shard_map/reduce_sum | solution.py:47
  267.2 0.0 all-reduce.10.cloned.1.call-update
  267.2 0.0 reduce-scatter.2.cloned.1.call-start
  267.3 32.9 %all-reduce.10.cloned.1.call-done = f32[16384]{0:T(1024)} async-done(((f32[16384]{0:T(1024)}), f32[16384]{0:T(1024)}) %all-reduce.10.cloned.1.call-update) | async-done | bytes 65552 | tf_op jit(solution)/shard_map/psum | solution.py:48
  300.2 0.9 broadcast_divide_fusion
  301.0 20.9 %multiply_reduce_fusion.5 = f32[1024]{0:T(1024)S(1)} fusion(f32[1024,16384]{1,0:T(8,128)} %get-tuple-element.7, f32[16384]{0:T(1024)S(1)} %broadcast_divide_fusion), kind=kLoop, calls=%fused_computation.8 | loop fusion | flops 33553408 | bytes 67178496 | tf_op jit(solution)/shard_map/reduce_sum | solution.py:49
  321.9 11.8 %psum.55 = f32[1024]{0:T(1024)S(1)} all-reduce(f32[1024]{0:T(1024)S(1)} %multiply_reduce_fusion.5), channel_id=1, replica_groups=mesh['rows'=4,'protos'=8] {'protos'}, use_global_device_ids=true, to_apply=%region_16.0 | all-reduce | flops 1024 | bytes 8192 | tf_op jit(solution)/shard_map/psum | solution.py:50
  333.8 54.2 %multiply_reduce_fusion = (f32[1024]{0:T(1024)S(1)}, f32[1024]{0:T(1024)S(1)}, f32[1024,16384]{1,0:T(8,128)}) fusion(f32[1024,16384]{1,0:T(8,128)} %get-tuple-element.7, f32[1024]{0:T(1024)S(1)} %broadcast_divide_fusion.3, f32[16384]{0:T(1024)S(1)} %broadcast_divide_fusion, bf16[256,16384]{1,0:T(8,128)(2,1)} %param.5, f32[16384]{0:T(1024)S(1)} %add_sqrt_fusion, ...), kind=kOutput, calls=%fused_computation | convolution fusion | flops 8703965184 | bytes 143278080 | tf_op jit(solution)/shard_map/dot_general | solution.py:41
  387.9 12.1 %all-reduce.1 = (f32[1024]{0:T(1024)S(1)}, f32[1024]{0:T(1024)S(1)}) all-reduce(f32[1024]{0:T(1024)S(1)} %get-tuple-element.3, f32[1024]{0:T(1024)S(1)} %get-tuple-element.2), channel_id=1, replica_groups=mesh['rows'=4,'protos'=8] {'protos'}, use_global_device_ids=true, to_apply=%region_3.0 | all-reduce | flops 2048 | bytes 16384 | tf_op jit(solution)/shard_map/psum | solution.py:52
  400.0 0.0 copy-start.2
  400.0 0.0 copy-start.1
  400.0 46.9 %fusion.4 = f32[1024,256]{1,0:T(8,128)} fusion(f32[1024,16384]{1,0:T(8,128)} %get-tuple-element.7, f32[1024,16384]{1,0:T(8,128)} %get-tuple-element.8, f32[1024]{0:T(1024)S(1)} %broadcast_divide_fusion.3, f32[16384]{0:T(1024)S(1)} %broadcast_divide_fusion, f32[1024]{0:T(1024)S(1)} %get-tuple-element.4, bf16[256,16384]{1,0:T(8,128)(2,1)} %param.5, ...), kind=kOutput, calls=%fused_computation.15 | convolution fusion | flops 8703442944 | bytes 143794176 | tf_op jit(solution)/shard_map/dot_general | solution.py:62
  446.9 0.0 reduce-scatter.2.cloned.1.call-update
  446.9 0.0 copy-done.2
  446.9 0.6 dynamic-slice
  448.2 0.0 copy-done.1
  448.2 0.1 fusion.12
  448.3 0.6 dynamic-slice_subtract_fusion
  448.9 33.0 %reduce-scatter.2.cloned.1.call-done = f32[128,256]{1,0:T(8,128)} async-done(((f32[1024,256]{1,0:T(8,128)}), f32[128,256]{1,0:T(8,128)}) %reduce-scatter.2.cloned.1.call-update) | async-done | bytes 131088 | tf_op jit(solution)/shard_map/reduce_scatter | solution.py:61
  481.9 1.1 multiply_reduce_fusion.6
  483.0 1.7 subtract_divide_fusion
  (8 shorter events, 0.1 us)
Async XLA Ops:
  7.2 116.9 %all-reduce.6.cloned.1.call-start = ((), (), s32[]{:S(2)}) async-start(), calls=%async_computation.1 | async-start | bytes 131072 | tf_op jit(solution)/shard_map/psum | solution.py:48
  24.4 65.3 %copy-start = (bf16[128,256]{1,0:T(8,128)(2,1)S(1)}, bf16[128,256]{1,0:T(8,128)(2,1)}, u32[]{:S(2)}) copy-start(bf16[128,256]{1,0:T(8,128)(2,1)} %param.4) | copy-start | bytes 196612
  89.6 122.5 %all-reduce.8.cloned.1.call-start = ((), (), s32[]{:S(2)}) async-start(), calls=%async_computation.2 | async-start | bytes 131072 | tf_op jit(solution)/shard_map/psum | solution.py:48
  179.2 121.0 %all-reduce.10.cloned.1.call-start = ((), (), s32[]{:S(2)}) async-start(), calls=%async_computation.3 | async-start | bytes 131072 | tf_op jit(solution)/shard_map/psum | solution.py:48
  267.2 214.7 %reduce-scatter.2.cloned.1.call-start = ((), (), s32[]{:S(2)}) async-start(), calls=%async_computation.4 | async-start | bytes 1179648 | tf_op jit(solution)/shard_map/reduce_scatter | solution.py:61
  400.0 46.9 %copy-start.2 = (u32[32]{0:T(128)S(1)}, u32[32]{0:T(128)}, u32[]{:S(2)}) copy-start(u32[32]{0:T(128)} %constant.29) | copy-start | bytes 388
  400.0 48.2 %copy-start.1 = (bf16[128,256]{1,0:T(8,128)(2,1)S(1)}, bf16[128,256]{1,0:T(8,128)(2,1)}, u32[]{:S(2)}) copy-start(bf16[128,256]{1,0:T(8,128)(2,1)} %param.4) | copy-start | bytes 196612
Sparse Core Ops, SparseCore 0:
  89.7 34.2 all-reduce.5
  179.3 32.7 all-reduce.7
  267.3 32.7 all-reduce.9
  447.0 34.8 reduce-scatter.1
where the time goes:
time: 492 us; the launch traced here: 491 us
  matrix products  166 us (34%)
  waiting for transfers between devices  123 us (25%)
  other arithmetic  117 us (24%)
  blocking collectives  68.9 us (14%)
  between operations  14.6 us (3%)
    psum x3, waiting for transfers between devices, on_device(): inverse = 1.0 / lax.psum(col_part, 'rows')  90.2 us
    dot_general x1, matrix products, on_device(): jnp.dot(teacher_unit, proto_unit, precision=lax.Precision.HIGHEST, prefer...  65.2 us
    reduce_sum x3, other arithmetic, on_device(): row_part = jnp.sum(teacher_exp * inverse[None, :], axis=1)  62.7 us
    dot_general x1, matrix products, on_device(): jnp.dot(student_unit, proto_half, preferred_element_type=jnp.float32)  54.2 us
    dot_general x1, matrix products, on_device(): lax.dot_general(signal, proto_half, (((1,), (1,)), ((), ())), preferred_e...  46.9 us
    reduce_sum x3, other arithmetic, on_device(): col_part = jnp.sum(teacher_exp * weights[:, None], axis=0)  43.2 us
    psum x3, blocking collectives, on_device(): row_total = lax.psum(row_part, 'protos')  35.5 us
    reduce_scatter x1, waiting for transfers between devices, on_device(): lax.psum_scatter(lax.dot_general(signal, proto_half, (((1,), (1,)), ((),...  33 us
  transfers between devices with their start and end apart: 4, of which 4 were waited for; matrix products, arithmetic and copies ran while one was open for 0% of the time, Pallas kernels for 0%

commit v1 on v0

v1 whole, which is shorter than its diff:
```python
import functools
import math

import jax
import jax.numpy as jnp
from jax import lax
from jax.experimental import pallas as pl
from jax.experimental.pallas import tpu as pltpu
from jax.sharding import PartitionSpec as P

EPSILON = 1e-06
TEACHER_TEMP = 0.04
STUDENT_TEMP = 0.1
LOG2E = math.log2(math.e)
F32 = jnp.float32
BF16 = jnp.bfloat16
MIB = 1 << 20
NT = (((1,), (1,)), ((), ()))
VMEM = pl.BlockSpec(memory_space=pltpu.VMEM)
PIECES = 8


def call(body, outs, args, scratch=(), vmem=4, flops=0, aliases={}):
    many = isinstance(outs, list)
    made = pl.pallas_call(
        body,
        out_shape=outs,
        in_specs=[VMEM] * len(args),
        out_specs=[VMEM] * len(outs) if many else VMEM,
        scratch_shapes=list(scratch),
        input_output_aliases=aliases,
        compiler_params=pltpu.CompilerParams(vmem_limit_bytes=vmem * MIB),
        cost_estimate=pl.CostEstimate(flops=flops, bytes_accessed=0, transcendentals=0),
    )
    return made(*[pltpu.with_memory_space_constraint(arg, pltpu.VMEM) for arg in args])


def aligned(index, size):
    return pl.ds(pl.multiple_of(index, size), size)


def norms_of(rows):
    floats = rows.astype(F32)
    return floats, jnp.sqrt(jnp.sum(floats * floats, axis=1, keepdims=True) + EPSILON)


def as_column(row):
    size = row.shape[1]
    if size < 128:
        row = jnp.concatenate([row, jnp.zeros((1, 128 - size), F32)], axis=1)
    return jnp.transpose(jnp.broadcast_to(row, (128, 128)))[:size]


def lane_groups(values):
    parts = [values[:, s : s + 128] for s in range(0, values.shape[1], 128)]
    while len(parts) > 1:
        rest = parts[len(parts) // 2 * 2 :]
        parts = [a + b for a, b in zip(parts[::2], parts[1::2])] + rest
    return parts[0]


def wide(column, width):
    return jnp.concatenate([column] * (width // 128), axis=1)


def fold(flat_ref, out_ref):
    for s in range(out_ref.shape[0]):
        out_ref[s : s + 1, :] = flat_ref[:, s * 128 : (s + 1) * 128]


def unfold(values, flat_ref):
    for s in range(values.shape[0]):
        flat_ref[:, s * 128 : (s + 1) * 128] = values[s : s + 1, :]


def rows_out(acc_ref, row_ref):
    for s in range(row_ref.shape[0]):
        block = jnp.transpose(acc_ref[s * 128 : (s + 1) * 128, :])
        row_ref[s : s + 1, :] = jnp.sum(block, axis=0, keepdims=True)


def prep_body(width, p_ref, half_ref, scale_ref):
    def step(i, _):
        cols = aligned(i * width, width)
        floats = p_ref[:, cols].astype(F32)
        scale = lax.rsqrt(jnp.sum(floats * floats, axis=0, keepdims=True) + EPSILON)
        half_ref[:, cols] = (floats * scale).astype(BF16)
        scale_ref[:, cols] = scale
        return 0

    lax.fori_loop(0, p_ref.shape[1] // width, step, 0)


def exp_body(width, chunk, slots, *refs):
    parts, (p_ref, scale_ref, e_ref, col_ref, unit_ref, t_ref, a_ref, flat_ref) = refs[:slots], refs[slots:]
    rows, cols_all = e_ref.shape
    size = rows // slots
    for m, part in enumerate(parts):
        here = slice(m * size, (m + 1) * size)
        teacher = part[0:size, :]
        t_ref[here, :] = teacher
        a_ref[here, :] = jnp.broadcast_to((LOG2E / TEACHER_TEMP) / norms_of(teacher)[1], (size, 128))
        floats, norm = norms_of(part[size:, :])
        unit_ref[here, :] = (floats / norm).astype(BF16)

    def step(i, _):
        for n in range(width // 256):
            cols = aligned(i * width + n * 256, 256)
            p = p_ref[:, cols]
            scale = scale_ref[:, cols]
            acc = jnp.zeros((8, 256), F32)
            for r in range(0, rows, chunk):
                d = jnp.dot(t_ref[r : r + chunk, :], p, preferred_element_type=F32)
                e = jnp.exp2(d * wide(a_ref[r : r + chunk, :], 256) * scale)
                e_ref[r : r + chunk, cols] = e.astype(BF16)
                acc = acc + jnp.sum(e.reshape(chunk // 8, 8, 256), axis=0)
            flat_ref[:, cols] = jnp.sum(acc, axis=0, keepdims=True)
        return 0

    lax.fori_loop(0, cols_all // width, step, 0)
    fold(flat_ref, col_ref)


def rowsum_body(width, group, chunk, core_lanes, e_ref, one_ref, two_ref, inv_ref, row_ref, swap_ref, acc_ref, flat_ref):
    rows, cols_all = e_ref.shape
    inv = 1.0 / (one_ref[...] + two_ref[...])
    inv_ref[...] = inv
    unfold(inv, flat_ref)
    acc_ref[...] = jnp.zeros_like(acc_ref)

    def step(i, _):
        for r in range(0, rows, chunk):
            acc = acc_ref[r : r + chunk, :]
            for n in range(width // group):
                cols = aligned(i * width + n * group, group)
                acc = acc + lane_groups(e_ref[r : r + chunk, cols].astype(F32) * flat_ref[:, cols])
            acc_ref[r : r + chunk, :] = acc
        return 0

    lax.fori_loop(0, cols_all // width, step, 0)
    rows_out(acc_ref, row_ref)
    if core_lanes == 128:
        for s in range(row_ref.shape[0]):
            swap_ref[s : s + 1, :] = row_ref[s ^ 1 : (s ^ 1) + 1, :]
    else:
        held = row_ref[...]
        swap_ref[...] = jnp.concatenate([held[:, core_lanes:], held[:, :core_lanes]], axis=1)


def colsum_body(width, size, e_ref, *refs):
    parts, (col_ref, w_ref, flat_ref) = refs[:-3], refs[-3:]
    rows, cols_all = e_ref.shape
    for s in range(rows // 128):
        total = parts[0][s : s + 1, :]
        for j, part in enumerate(parts[1:], 1):
            from_ = s ^ (2 * j * size // 128)
            total = total + part[from_ : from_ + 1, :]
        w = 1.0 / total
        high = w.astype(BF16).astype(F32)
        low = w - high
        both = jnp.concatenate([high, low, jnp.zeros((14, 128), F32)], axis=0)
        w_ref[:, s * 128 : (s + 1) * 128] = both.astype(BF16)

    def step(i, _):
        cols = aligned(i * width, width)
        sums = jnp.dot(w_ref[...], e_ref[:, cols], preferred_element_type=F32)
        flat_ref[:, cols] = sums[0:1, :] + sums[1:2, :]
        return 0

    lax.fori_loop(0, cols_all // width, step, 0)
    fold(flat_ref, col_ref)


def student_body(width, group, chunk, first, last, unit_ref, half_ref, *refs):
    grad_ref, acc_ref = refs[-2:]
    rows = unit_ref.shape[0]
    if first == 0:
        grad_ref[...] = jnp.zeros_like(grad_ref)
        acc_ref[...] = jnp.zeros_like(acc_ref)

    def step(i, _):
        for n in range(width // group):
            cols = aligned(first + i * width + n * group, group)
            q = half_ref[:, cols]
            for r in range(0, rows, chunk):
                d = jnp.dot(unit_ref[r : r + chunk, :], q, preferred_element_type=F32)
                x = jnp.exp2(d * (LOG2E / STUDENT_TEMP))
                grad_ref[r : r + chunk, :] += lax.dot_general(x.astype(BF16), q, NT, preferred_element_type=F32)
                acc_ref[r : r + chunk, :] += lane_groups(x)
        return 0

    lax.fori_loop(0, (last - first) // width, step, 0)


def last_body(width, chunk, slots, e_ref, inv_ref, half_ref, row_ref, grad_ref, sum_ref, even_ref, odd_ref, b_ref, flat_ref, s_ref):
    rows, cols_all = e_ref.shape
    size = rows // slots
    unfold(inv_ref[...], flat_ref)
    rows_out(sum_ref, s_ref)
    b_ref[...] = jnp.zeros_like(b_ref)

    def step(i, _):
        cols = aligned(i * width, width)
        q = (half_ref[:, cols].astype(F32) * flat_ref[:, cols]).astype(BF16)
        for r in range(0, rows, chunk):
            b_ref[r : r + chunk, :] += lax.dot_general(e_ref[r : r + chunk, cols], q, NT, preferred_element_type=F32)
        return 0

    lax.fori_loop(0, cols_all // width, step, 0)
    depth = grad_ref.shape[1]
    for m in range(slots):
        out = odd_ref if m % 2 else even_ref
        here = slice(m * size, (m + 1) * size)
        out[m // 2, 0:size, 0:depth] = grad_ref[here, :]
        out[m // 2, 0:size, depth:] = b_ref[here, :]
        out[m // 2, size:, :] = jnp.zeros((8, 2 * depth), F32)
        s, lane = divmod(m * size, 128)
        out[m // 2, size : size + 1, 0:size] = s_ref[s : s + 1, lane : lane + size]
        out[m // 2, size : size + 1, depth : depth + size] = row_ref[s : s + 1, lane : lane + size]


def final_body(student_ref, *refs):
    parts, (grads_ref, loss_ref) = refs[:-2], refs[-2:]
    size, depth = student_ref.shape
    total = parts[0][...]
    for part in parts[1:]:
        total = total + part[...]
    s_row = total[size : size + 1, 0:size]
    r_row = total[size : size + 1, depth : depth + size]
    a = total[0:size, 0:depth] / wide(as_column(s_row), depth)
    b = total[0:size, depth:] / wide(as_column(r_row), depth)
    floats, norm = norms_of(student_ref[...])
    unit = floats / norm
    direction = (a - b) / STUDENT_TEMP
    radial = jnp.sum(unit * direction, axis=1, keepdims=True)
    grads_ref[...] = (direction - unit * radial) / norm
    product = unit.astype(BF16).astype(F32) * b
    cross = jnp.sum(product, axis=1, keepdims=True) / STUDENT_TEMP
    cross = jnp.broadcast_to(cross, (size, 128))
    if size < 128:
        cross = jnp.concatenate([cross, jnp.zeros((128 - size, 128), F32)], axis=0)
    loss_ref[...] = jnp.log(s_row) - jnp.transpose(cross)[0:1, 0:size]


def on_device(row_devices, proto_devices, teacher_rows, student_rows, prototypes):
    size, depth = teacher_rows.shape
    cols = prototypes.shape[1]
    rows = size * proto_devices
    chips = range(2, proto_devices, 2)
    lines, blocks = rows // 128, cols // 128
    vm = pltpu.VMEM

    def swap(values, mask, axis="protos", count=proto_devices):
        return lax.ppermute(values, axis, [(i, i ^ mask) for i in range(count)])

    def over_rows(values):
        mask = 1
        while True:
            other = swap(values, mask, "rows", row_devices)
            mask *= 2
            if mask >= row_devices:
                return values, other
            values = values + other

    both = jnp.concatenate([teacher_rows, student_rows], axis=0)
    even = [both] + [swap(both, mask) for mask in chips]
    odd = [swap(part, 1) for part in even]
    parts = [part for pair in zip(even, odd) for part in pair]

    half, scale = call(functools.partial(prep_body, 512), [vm((depth, cols), BF16), vm((1, cols), F32)], [prototypes])
    exps, col, unit = call(
        functools.partial(exp_body, 2048, 256, proto_devices),
        [vm((rows, cols), BF16), vm((blocks, 128), F32), vm((rows, depth), BF16)],
        parts + [prototypes, scale],
        [pltpu.VMEM((rows, depth), BF16), pltpu.VMEM((rows, 128), F32), pltpu.VMEM((1, cols), F32)],
        vmem=6,
    )

    work = 4 * rows * cols * depth // PIECES

    def student(piece, held):
        first, last = piece * cols // PIECES, (piece + 1) * cols // PIECES
        return call(
            functools.partial(student_body, min(2048, last - first), 1024, 256, first, last),
            [vm((rows, depth), F32), vm((rows, 128), F32)],
            [unit, half, *held],
            vmem=6,
            flops=work,
            aliases={2: 0, 3: 1} if held else {},
        )

    held = []
    for piece in range(PIECES):
        held = student(piece, held)

    for sweep in range(3):
        one, two = over_rows(col)
        inv, row, swapped = call(
            functools.partial(rowsum_body, 2048, 1024, 128, size),
            [vm((blocks, 128), F32), vm((lines, 128), F32), vm((lines, 128), F32)],
            [exps, one, two],
            [pltpu.VMEM((rows, 128), F32), pltpu.VMEM((1, cols), F32)],
        )
        if sweep == 2:
            break
        row = row + swap(swapped, 1)
        col = call(
            functools.partial(colsum_body, 4096, size),
            vm((blocks, 128), F32),
            [exps, row] + [swap(row, mask) for mask in chips],
            [pltpu.VMEM((16, rows), BF16), pltpu.VMEM((1, cols), F32)],
        )

    block = vm((proto_devices // 2, size + 8, 2 * depth), F32)
    stay, leave = call(
        functools.partial(last_body, 2048, 256, proto_devices),
        [block, block],
        [exps, inv, half, row, *held],
        [pltpu.VMEM((rows, depth), F32), pltpu.VMEM((1, cols), F32), pltpu.VMEM((lines, 128), F32)],
        vmem=6,
    )
    stay = stay + swap(leave, 1)
    sums = [stay[0]] + [swap(stay[mask // 2], mask) for mask in chips]
    grads, loss = call(
        final_body,
        [jax.ShapeDtypeStruct((size, depth), F32), jax.ShapeDtypeStruct((1, size), F32)],
        [student_rows] + sums,
    )
    return grads, loss.reshape(size)


def solution(mesh):
    in_specs = (P(("rows", "protos"), None), P(("rows", "protos"), None), P(None, "protos"))
    out_specs = (P(("rows", "protos"), None), P(("rows", "protos")))
    return jax.shard_map(
        functools.partial(on_device, mesh.shape["rows"], mesh.shape["protos"]),
        mesh=mesh,
        in_specs=in_specs,
        out_specs=out_specs,
        check_vma=False,
    )
```

time: 492 us -> 222 us (0.45)
  matrix products: 166 us -> 0 us
  other arithmetic: 117 us -> 0.26 us
  waiting for transfers between devices: 123 us -> 26.6 us
  local copies, waits for them, and re-layouts: 0.61 us -> 82.8 us
  Pallas kernels: 0 us -> 80.9 us
  blocking collectives: 68.9 us -> 0 us
  starting transfers between devices: 0.16 us -> 29.8 us
  between operations: 14.6 us -> 0.93 us
    dot_general x3 -> x0, matrix products: 166 us -> none  [the longest x1 65.2 us: on_device(): jnp.dot(teacher_unit, proto_unit, precision=lax.Precision.HIGHEST, prefer...]
    reduce_sum x11 -> x0, other arithmetic: 113 us -> none  [the longest x3 62.7 us: on_device(): row_part = jnp.sum(teacher_exp * inverse[None, :], axis=1)]
    psum x3 -> x0, waiting for transfers between devices: 90.2 us -> none  [on_device(): inverse = 1.0 / lax.psum(col_part, 'rows')]
    unnamed x7 -> x21, local copies, waits for them, and re-layouts: 0.6 us -> 81.9 us
    pallas_call x0 -> x17, Pallas kernels: none -> 80.9 us  [call(): made(*[pltpu.with_memory_space_constraint(arg, pltpu.VMEM) for arg in args])]
    psum x4 -> x0, blocking collectives: 47.6 us -> none  [the longest x3 35.5 us: on_device(): row_total = lax.psum(row_part, 'protos')]
    reduce_scatter x1 -> x0, waiting for transfers between devices: 33 us -> none  [on_device(): lax.psum_scatter(lax.dot_general(signal, proto_half, (((1,), (1,)), ((),...]
    ppermute x0 -> x25, starting transfers between devices: none -> 29.8 us  [swap(): return lax.ppermute(values, axis, [(i, i ^ mask) for i in range(count)])]
  transfers between devices with their start and end apart: 4 -> 25, of which waited for: 4 -> 10; matrix products, arithmetic and copies ran while one was open for 0% -> 0% of each run, Pallas kernels for 0% -> 11%
where the time goes in v1:
time: 222 us; the launch traced here: 221 us
  local copies, waits for them, and re-layouts  82.8 us (37%)
  Pallas kernels  80.9 us (36%)
  starting transfers between devices  29.8 us (13%)
  waiting for transfers between devices  26.6 us (12%)
    unnamed x21, local copies, waits for them, and re-layouts  81.9 us
    pallas_call x17, Pallas kernels, call(): made(*[pltpu.with_memory_space_constraint(arg, pltpu.VMEM) for arg in args])  80.9 us
    ppermute x25, starting transfers between devices, swap(): return lax.ppermute(values, axis, [(i, i ^ mask) for i in range(count)])  29.8 us
    ppermute x25, waiting for transfers between devices, swap(): return lax.ppermute(values, axis, [(i, i ^ mask) for i in range(count)])  26.6 us
  transfers between devices with their start and end apart: 25, of which 10 were waited for; matrix products, arithmetic and copies ran while one was open for 0% of the time, Pallas kernels for 11%

profile of v1, /device:TPU:0, one launch (start us, length us, event | category | flops | bytes accessed | tf_op | source)
XLA Modules:
  0.0 221.3 jit_solution(16613759944433317703)
XLA Ops:
  2.3 3.9 %collective-permute-start.5 = (bf16[256,256]{1,0:T(8,128)(2,1)S(1)}, bf16[256,256]{1,0:T(8,128)(2,1)S(1)}, u32[]{:S(2)}, u32[]{:S(2)}) collective-permute-start(bf16[256,256]{1,0:T(8,128)(2,1)S(1)} %constant_dynamic-update-slice_fusion.refs_0_), channel_id=1, source_target_pairs={{0,6},{1,7},{2,4},{3,5},{4,2},{5,3},{6,0},{7,1},{8,14},{9,15},{10,... | collective-permute-start | bytes 393224 | tf_op jit(solution)/shard_map/ppermute | solution.py:254
  6.8 3.3 %collective-permute-done.5.refs_6_ = bf16[256,256]{1,0:T(8,128)(2,1)S(1)} collective-permute-done((bf16[256,256]{1,0:T(8,128)(2,1)S(1)}, bf16[256,256]{1,0:T(8,128)(2,1)S(1)}, u32[]{:S(2)}, u32[]{:S(2)}) %collective-permute-start.5) | collective-permute-done | bytes 131104 | tf_op jit(solution)/shard_map/ppermute | solution.py:254
  10.1 2.4 %collective-permute-done.3.refs_4_ = bf16[256,256]{1,0:T(8,128)(2,1)S(1)} collective-permute-done((bf16[256,256]{1,0:T(8,128)(2,1)S(1)}, bf16[256,256]{1,0:T(8,128)(2,1)S(1)}, u32[]{:S(2)}, u32[]{:S(2)}) %collective-permute-start.3) | collective-permute-done | bytes 131104 | tf_op jit(solution)/shard_map/ppermute | solution.py:254
  13.0 3.4 %copy-done.7 = bf16[256,16384]{1,0:T(8,128)(2,1)S(1)} copy-done((bf16[256,16384]{1,0:T(8,128)(2,1)S(1)}, bf16[256,16384]{1,0:T(8,128)(2,1)}, u32[]{:S(2)}) %copy-start.7) | copy-done | bytes 8388632
  16.4 3.3 %shard_map.50 = (bf16[256,16384]{1,0:T(8,128)(2,1)S(1)}, f32[1,16384]{1,0:T(1,128)S(1)}) custom-call(bf16[256,16384]{1,0:T(8,128)(2,1)S(1)} %copy-done.7), custom_call_target="tpu_custom_call" | custom-call | tf_op jit(solution)/shard_map/pallas_call | solution.py:35
  19.8 3.4 %copy-done.8 = bf16[256,16384]{1,0:T(8,128)(2,1)S(1)} copy-done((bf16[256,16384]{1,0:T(8,128)(2,1)S(1)}, bf16[256,16384]{1,0:T(8,128)(2,1)}, u32[]{:S(2)}) %copy-start.8) | copy-done | bytes 8388632
  23.2 14.0 %shard_map.51 = (bf16[1024,16384]{1,0:T(8,128)(2,1)S(1)}, f32[128,128]{1,0:T(8,128)S(1)}, bf16[1024,256]{1,0:T(8,128)(2,1)S(1)}) custom-call(bf16[256,256]{1,0:T(8,128)(2,1)S(1)} %constant_dynamic-update-slice_fusion.refs_0_, bf16[256,256]{1,0:T(8,128)(2,1)S(1)} %collective-permute-done.refs_1_, bf16[256,256]{1,0:T(8,128)(2,1)S(1)} %collective-permute-done.1.refs_2_, ...), custom_call_target="tpu_custom_call" | custom-call | tf_op jit(solution)/shard_map/pallas_call | solution.py:35
  37.2 11.1 %copy-done = bf16[1024,16384]{1,0:T(8,128)(2,1)} copy-done((bf16[1024,16384]{1,0:T(8,128)(2,1)}, bf16[1024,16384]{1,0:T(8,128)(2,1)S(1)}, u32[]{:S(2)}) %copy-start) | copy-done | bytes 33554456
  48.2 1.8 collective-permute-start.7
  50.0 2.5 %collective-permute-done.7 = f32[128,128]{1,0:T(8,128)S(1)} collective-permute-done((f32[128,128]{1,0:T(8,128)S(1)}, f32[128,128]{1,0:T(8,128)S(1)}, u32[]{:S(2)}, u32[]{:S(2)}) %collective-permute-start.7) | collective-permute-done | bytes 65568 | tf_op jit(solution)/shard_map/ppermute | solution.py:254
  52.5 2.9 %collective-permute-start.8 = (f32[128,128]{1,0:T(8,128)S(1)}, f32[128,128]{1,0:T(8,128)S(1)}, u32[]{:S(2)}, u32[]{:S(2)}) collective-permute-start(f32[128,128]{1,0:T(8,128)S(1)} %add.18.one_ref), channel_id=1, source_target_pairs={{0,16},{8,24},{16,0},{24,8},{1,17},{9,25},{17,1},{25,9},{2,18},{10... | collective-permute-start | bytes 196616 | tf_op jit(solution)/shard_map/ppermute | solution.py:254
  55.3 2.4 %collective-permute-done.8.two_ref = f32[128,128]{1,0:T(8,128)S(1)} collective-permute-done((f32[128,128]{1,0:T(8,128)S(1)}, f32[128,128]{1,0:T(8,128)S(1)}, u32[]{:S(2)}, u32[]{:S(2)}) %collective-permute-start.8) | collective-permute-done | bytes 65568 | tf_op jit(solution)/shard_map/ppermute | solution.py:254
  57.7 10.5 %copy-done.1 = bf16[1024,16384]{1,0:T(8,128)(2,1)S(1)} copy-done((bf16[1024,16384]{1,0:T(8,128)(2,1)S(1)}, bf16[1024,16384]{1,0:T(8,128)(2,1)}, u32[]{:S(2)}) %copy-start.1) | copy-done | bytes 33554456
  68.3 7.2 %shard_map.52 = (f32[128,128]{1,0:T(8,128)}, f32[8,128]{1,0:T(8,128)S(1)}, f32[8,128]{1,0:T(8,128)S(1)}) custom-call(bf16[1024,16384]{1,0:T(8,128)(2,1)S(1)} %copy-done.1, f32[128,128]{1,0:T(8,128)S(1)} %add.18.one_ref, f32[128,128]{1,0:T(8,128)S(1)} %collective-permute-done.8.two_ref), custom_call_target="tpu_custom_call" | custom-call | tf_op jit(solution)/shard_map/pallas_call | solution.py:35
  75.5 2.5 %shard_map.57 = (f32[1024,256]{1,0:T(8,128)S(1)}, f32[1024,128]{1,0:T(8,128)S(1)}) custom-call(bf16[1024,256]{1,0:T(8,128)(2,1)S(1)} %get-tuple-element.43.unit_ref, bf16[256,16384]{1,0:T(8,128)(2,1)S(1)} %get-tuple-element.41.half_ref), custom_call_target="tpu_custom_call" | custom-call | flops 2147483648 | tf_op jit(solution)/shard_map/pallas_call | solution.py:35
  78.0 1.8 collective-permute-start.12
  79.9 1.4 collective-permute-start.11
  81.6 2.5 %shard_map.58 = (f32[1024,256]{1,0:T(8,128)S(1)}, f32[1024,128]{1,0:T(8,128)S(1)}) custom-call(bf16[1024,256]{1,0:T(8,128)(2,1)S(1)} %get-tuple-element.43.unit_ref, bf16[256,16384]{1,0:T(8,128)(2,1)S(1)} %get-tuple-element.41.half_ref, f32[1024,256]{1,0:T(8,128)S(1)} %get-tuple-element.44.refs_0_, ...), custom_call_target="tpu_custom_call", output_to_operand_aliasing={{0}: (2, {}), {1}: (3, {})} | custom-call | flops 2147483648 | tf_op jit(solution)/shard_map/pallas_call | solution.py:35
  84.8 10.5 %copy-done.2 = bf16[1024,16384]{1,0:T(8,128)(2,1)S(1)} copy-done((bf16[1024,16384]{1,0:T(8,128)(2,1)S(1)}, bf16[1024,16384]{1,0:T(8,128)(2,1)}, u32[]{:S(2)}) %copy-start.2) | copy-done | bytes 33554456
  95.4 4.9 %shard_map.53 = f32[128,128]{1,0:T(8,128)S(1)} custom-call(bf16[1024,16384]{1,0:T(8,128)(2,1)S(1)} %copy-done.2, f32[8,128]{1,0:T(8,128)S(1)} %add.19.refs_0_, f32[8,128]{1,0:T(8,128)S(1)} %collective-permute-done.10.refs_1_, f32[8,128]{1,0:T(8,128)S(1)} %collective-permute-done.11.refs_2_, f32[8,128]{1,0:T(8,128)S(1)} %collective-permute-done.12.refs_3_), custom_call_target="tpu_custom_call" | custom-call | tf_op jit(solution)/shard_map/pallas_call | solution.py:35
  100.3 1.7 collective-permute-start.13
  102.0 2.5 %shard_map.59 = (f32[1024,256]{1,0:T(8,128)S(1)}, f32[1024,128]{1,0:T(8,128)S(1)}) custom-call(bf16[1024,256]{1,0:T(8,128)(2,1)S(1)} %get-tuple-element.43.unit_ref, bf16[256,16384]{1,0:T(8,128)(2,1)S(1)} %get-tuple-element.41.half_ref, f32[1024,256]{1,0:T(8,128)S(1)} %get-tuple-element.46.refs_0_, ...), custom_call_target="tpu_custom_call", output_to_operand_aliasing={{0}: (2, {}), {1}: (3, {})} | custom-call | flops 2147483648 | tf_op jit(solution)/shard_map/pallas_call | solution.py:35
  104.7 3.1 %collective-permute-start.14 = (f32[128,128]{1,0:T(8,128)S(1)}, f32[128,128]{1,0:T(8,128)S(1)}, u32[]{:S(2)}, u32[]{:S(2)}) collective-permute-start(f32[128,128]{1,0:T(8,128)S(1)} %add.20.one_ref), channel_id=1, source_target_pairs={{0,16},{8,24},{16,0},{24,8},{1,17},{9,25},{17,1},{25,9},{2,18},{10... | collective-permute-start | bytes 196616 | tf_op jit(solution)/shard_map/ppermute | solution.py:254
  107.8 2.5 %shard_map.60 = (f32[1024,256]{1,0:T(8,128)S(1)}, f32[1024,128]{1,0:T(8,128)S(1)}) custom-call(bf16[1024,256]{1,0:T(8,128)(2,1)S(1)} %get-tuple-element.43.unit_ref, bf16[256,16384]{1,0:T(8,128)(2,1)S(1)} %get-tuple-element.41.half_ref, f32[1024,256]{1,0:T(8,128)S(1)} %get-tuple-element.48.refs_0_, ...), custom_call_target="tpu_custom_call", output_to_operand_aliasing={{0}: (2, {}), {1}: (3, {})} | custom-call | flops 2147483648 | tf_op jit(solution)/shard_map/pallas_call | solution.py:35
  110.3 10.5 %copy-done.3 = bf16[1024,16384]{1,0:T(8,128)(2,1)S(1)} copy-done((bf16[1024,16384]{1,0:T(8,128)(2,1)S(1)}, bf16[1024,16384]{1,0:T(8,128)(2,1)}, u32[]{:S(2)}) %copy-start.3) | copy-done | bytes 33554456
  120.9 7.2 %shard_map.54 = (f32[128,128]{1,0:T(8,128)}, f32[8,128]{1,0:T(8,128)S(1)}, f32[8,128]{1,0:T(8,128)S(1)}) custom-call(bf16[1024,16384]{1,0:T(8,128)(2,1)S(1)} %copy-done.3, f32[128,128]{1,0:T(8,128)S(1)} %add.20.one_ref, f32[128,128]{1,0:T(8,128)S(1)} %collective-permute-done.14.two_ref), custom_call_target="tpu_custom_call" | custom-call | tf_op jit(solution)/shard_map/pallas_call | solution.py:35
  128.1 2.5 %shard_map.61 = (f32[1024,256]{1,0:T(8,128)S(1)}, f32[1024,128]{1,0:T(8,128)S(1)}) custom-call(bf16[1024,256]{1,0:T(8,128)(2,1)S(1)} %get-tuple-element.43.unit_ref, bf16[256,16384]{1,0:T(8,128)(2,1)S(1)} %get-tuple-element.41.half_ref, f32[1024,256]{1,0:T(8,128)S(1)} %get-tuple-element.50.refs_0_, ...), custom_call_target="tpu_custom_call", output_to_operand_aliasing={{0}: (2, {}), {1}: (3, {})} | custom-call | flops 2147483648 | tf_op jit(solution)/shard_map/pallas_call | solution.py:35
  130.6 1.5 collective-permute-start.18
  132.2 1.0 collective-permute-start.17
  133.1 1.1 collective-permute-start.16
  134.2 2.5 %shard_map.62 = (f32[1024,256]{1,0:T(8,128)S(1)}, f32[1024,128]{1,0:T(8,128)S(1)}) custom-call(bf16[1024,256]{1,0:T(8,128)(2,1)S(1)} %get-tuple-element.43.unit_ref, bf16[256,16384]{1,0:T(8,128)(2,1)S(1)} %get-tuple-element.41.half_ref, f32[1024,256]{1,0:T(8,128)S(1)} %get-tuple-element.52.refs_0_, ...), custom_call_target="tpu_custom_call", output_to_operand_aliasing={{0}: (2, {}), {1}: (3, {})} | custom-call | flops 2147483648 | tf_op jit(solution)/shard_map/pallas_call | solution.py:35
  136.7 10.5 %copy-done.4 = bf16[1024,16384]{1,0:T(8,128)(2,1)S(1)} copy-done((bf16[1024,16384]{1,0:T(8,128)(2,1)S(1)}, bf16[1024,16384]{1,0:T(8,128)(2,1)}, u32[]{:S(2)}) %copy-start.4) | copy-done | bytes 33554456
  147.3 5.1 %shard_map.55 = f32[128,128]{1,0:T(8,128)S(1)} custom-call(bf16[1024,16384]{1,0:T(8,128)(2,1)S(1)} %copy-done.4, f32[8,128]{1,0:T(8,128)S(1)} %add.21.refs_0_, f32[8,128]{1,0:T(8,128)S(1)} %collective-permute-done.16.refs_1_, f32[8,128]{1,0:T(8,128)S(1)} %collective-permute-done.17.refs_2_, f32[8,128]{1,0:T(8,128)S(1)} %collective-permute-done.18.refs_3_), custom_call_target="tpu_custom_call" | custom-call | tf_op jit(solution)/shard_map/pallas_call | solution.py:35
  152.4 1.8 collective-permute-start.19
  154.2 2.5 %shard_map.63 = (f32[1024,256]{1,0:T(8,128)S(1)}, f32[1024,128]{1,0:T(8,128)S(1)}) custom-call(bf16[1024,256]{1,0:T(8,128)(2,1)S(1)} %get-tuple-element.43.unit_ref, bf16[256,16384]{1,0:T(8,128)(2,1)S(1)} %get-tuple-element.41.half_ref, f32[1024,256]{1,0:T(8,128)S(1)} %get-tuple-element.54.refs_0_, ...), custom_call_target="tpu_custom_call", output_to_operand_aliasing={{0}: (2, {}), {1}: (3, {})} | custom-call | flops 2147483648 | tf_op jit(solution)/shard_map/pallas_call | solution.py:35
  156.7 3.1 %collective-permute-start.20 = (f32[128,128]{1,0:T(8,128)S(1)}, f32[128,128]{1,0:T(8,128)S(1)}, u32[]{:S(2)}, u32[]{:S(2)}) collective-permute-start(f32[128,128]{1,0:T(8,128)S(1)} %add.22.one_ref), channel_id=1, source_target_pairs={{0,16},{8,24},{16,0},{24,8},{1,17},{9,25},{17,1},{25,9},{2,18},{10... | collective-permute-start | bytes 196616 | tf_op jit(solution)/shard_map/ppermute | solution.py:254
  159.9 2.5 %shard_map.64 = (f32[1024,256]{1,0:T(8,128)S(1)}, f32[1024,128]{1,0:T(8,128)S(1)}) custom-call(bf16[1024,256]{1,0:T(8,128)(2,1)S(1)} %get-tuple-element.43.unit_ref, bf16[256,16384]{1,0:T(8,128)(2,1)S(1)} %get-tuple-element.41.half_ref, f32[1024,256]{1,0:T(8,128)S(1)} %get-tuple-element.56.refs_0_, ...), custom_call_target="tpu_custom_call", output_to_operand_aliasing={{0}: (2, {}), {1}: (3, {})} | custom-call | flops 2147483648 | tf_op jit(solution)/shard_map/pallas_call | solution.py:35
  162.4 10.5 %copy-done.5 = bf16[1024,16384]{1,0:T(8,128)(2,1)S(1)} copy-done((bf16[1024,16384]{1,0:T(8,128)(2,1)S(1)}, bf16[1024,16384]{1,0:T(8,128)(2,1)}, u32[]{:S(2)}) %copy-start.5) | copy-done | bytes 33554456
  172.9 7.4 %shard_map.56 = (f32[128,128]{1,0:T(8,128)S(1)}, f32[8,128]{1,0:T(8,128)S(1)}, f32[8,128]{1,0:T(8,128)}) custom-call(bf16[1024,16384]{1,0:T(8,128)(2,1)S(1)} %copy-done.5, f32[128,128]{1,0:T(8,128)S(1)} %add.22.one_ref, f32[128,128]{1,0:T(8,128)S(1)} %collective-permute-done.20.two_ref), custom_call_target="tpu_custom_call" | custom-call | tf_op jit(solution)/shard_map/pallas_call | solution.py:35
  180.4 10.5 %copy-done.6 = bf16[1024,16384]{1,0:T(8,128)(2,1)S(1)} copy-done((bf16[1024,16384]{1,0:T(8,128)(2,1)S(1)}, bf16[1024,16384]{1,0:T(8,128)(2,1)}, u32[]{:S(2)}) %copy-start.6) | copy-done | bytes 33554456
  190.9 10.7 %shard_map.65 = (f32[4,136,512]{2,1,0:T(8,128)S(1)}, f32[4,136,512]{2,1,0:T(8,128)S(1)}) custom-call(bf16[1024,16384]{1,0:T(8,128)(2,1)S(1)} %copy-done.6, f32[128,128]{1,0:T(8,128)S(1)} %get-tuple-element.40.inv_ref, bf16[256,16384]{1,0:T(8,128)(2,1)S(1)} %get-tuple-element.41.half_ref, f32[8,128]{1,0:T(8,128)S(1)} %get-tuple-element.42.row_ref, ...), custom_call_target="tpu_custom_call" | custom-call | tf_op jit(solution)/shard_map/pallas_call | solution.py:35
  201.7 2.7 %collective-permute-done.21 = f32[4,136,512]{2,1,0:T(8,128)S(1)} collective-permute-done((f32[4,136,512]{2,1,0:T(8,128)S(1)}, f32[4,136,512]{2,1,0:T(8,128)S(1)}, u32[]{:S(2)}, u32[]{:S(2)}) %collective-permute-start.21) | collective-permute-done | bytes 1114144 | tf_op jit(solution)/shard_map/ppermute | solution.py:254
  204.8 1.5 collective-permute-start.24
  206.3 1.1 collective-permute-start.23
  207.4 1.0 collective-permute-start.22
  208.3 7.0 %collective-permute-done.24.refs_3_ = f32[136,512]{1,0:T(8,128)S(1)} collective-permute-done((f32[136,512]{1,0:T(8,128)S(1)}, f32[136,512]{1,0:T(8,128)S(1)}, u32[]{:S(2)}, u32[]{:S(2)}) %collective-permute-start.24) | collective-permute-done | bytes 278560 | tf_op jit(solution)/shard_map/ppermute | solution.py:254
  215.3 5.1 %collective-permute-done.23.refs_2_ = f32[136,512]{1,0:T(8,128)S(1)} collective-permute-done((f32[136,512]{1,0:T(8,128)S(1)}, f32[136,512]{1,0:T(8,128)S(1)}, u32[]{:S(2)}, u32[]{:S(2)}) %collective-permute-start.23) | collective-permute-done | bytes 278560 | tf_op jit(solution)/shard_map/ppermute | solution.py:254
  220.4 0.9 shard_map.66
  (48 shorter events, 4.5 us)
Async XLA Ops:
  2.3 7.8 %collective-permute-start.5 = (bf16[256,256]{1,0:T(8,128)(2,1)S(1)}, bf16[256,256]{1,0:T(8,128)(2,1)S(1)}, u32[]{:S(2)}, u32[]{:S(2)}) collective-permute-start(bf16[256,256]{1,0:T(8,128)(2,1)S(1)} %constant_dynamic-update-slice_fusion.refs_0_), channel_id=1, source_target_pairs={{0,6},{1,7},{2,4},{3,5},{4,2},{5,3},{6,0},{7,1},{8,14},{9,15},{10,... | collective-permute-start | bytes 393224 | tf_op jit(solution)/shard_map/ppermute | solution.py:254
  6.2 6.3 %collective-permute-start.3 = (bf16[256,256]{1,0:T(8,128)(2,1)S(1)}, bf16[256,256]{1,0:T(8,128)(2,1)S(1)}, u32[]{:S(2)}, u32[]{:S(2)}) collective-permute-start(bf16[256,256]{1,0:T(8,128)(2,1)S(1)} %constant_dynamic-update-slice_fusion.refs_0_), channel_id=1, source_target_pairs={{0,4},{1,5},{2,6},{3,7},{4,0},{5,1},{6,2},{7,3},{8,12},{9,13},{10,... | collective-permute-start | bytes 393224 | tf_op jit(solution)/shard_map/ppermute | solution.py:254
  6.7 6.0 %collective-permute-start.1 = (bf16[256,256]{1,0:T(8,128)(2,1)S(1)}, bf16[256,256]{1,0:T(8,128)(2,1)S(1)}, u32[]{:S(2)}, u32[]{:S(2)}) collective-permute-start(bf16[256,256]{1,0:T(8,128)(2,1)S(1)} %constant_dynamic-update-slice_fusion.refs_0_), channel_id=1, source_target_pairs={{0,2},{1,3},{2,0},{3,1},{4,6},{5,7},{6,4},{7,5},{8,10},{9,11},{10,... | collective-permute-start | bytes 393224 | tf_op jit(solution)/shard_map/ppermute | solution.py:254
  6.8 13.0 %collective-permute-start = (bf16[256,256]{1,0:T(8,128)(2,1)S(1)}, bf16[256,256]{1,0:T(8,128)(2,1)S(1)}, u32[]{:S(2)}, u32[]{:S(2)}) collective-permute-start(bf16[256,256]{1,0:T(8,128)(2,1)S(1)} %constant_dynamic-update-slice_fusion.refs_0_), channel_id=1, source_target_pairs={{0,1},{1,0},{2,3},{3,2},{4,5},{5,4},{6,7},{7,6},{8,9},{9,8},{10,11... | collective-permute-start | bytes 393224 | tf_op jit(solution)/shard_map/ppermute | solution.py:254
  10.1 9.6 %collective-permute-start.6 = (bf16[256,256]{1,0:T(8,128)(2,1)S(1)}, bf16[256,256]{1,0:T(8,128)(2,1)S(1)}, u32[]{:S(2)}, u32[]{:S(2)}) collective-permute-start(bf16[256,256]{1,0:T(8,128)(2,1)S(1)} %collective-permute-done.5.refs_6_), channel_id=1, source_target_pairs={{0,1},{1,0},{2,3},{3,2},{4,5},{5,4},{6,7},{7,6},{8,9},{9,8},{10,11... | collective-permute-start | bytes 393224 | tf_op jit(solution)/shard_map/ppermute | solution.py:254
  12.5 7.3 %collective-permute-start.4 = (bf16[256,256]{1,0:T(8,128)(2,1)S(1)}, bf16[256,256]{1,0:T(8,128)(2,1)S(1)}, u32[]{:S(2)}, u32[]{:S(2)}) collective-permute-start(bf16[256,256]{1,0:T(8,128)(2,1)S(1)} %collective-permute-done.3.refs_4_), channel_id=1, source_target_pairs={{0,1},{1,0},{2,3},{3,2},{4,5},{5,4},{6,7},{7,6},{8,9},{9,8},{10,11... | collective-permute-start | bytes 393224 | tf_op jit(solution)/shard_map/ppermute | solution.py:254
  12.8 7.0 %collective-permute-start.2 = (bf16[256,256]{1,0:T(8,128)(2,1)S(1)}, bf16[256,256]{1,0:T(8,128)(2,1)S(1)}, u32[]{:S(2)}, u32[]{:S(2)}) collective-permute-start(bf16[256,256]{1,0:T(8,128)(2,1)S(1)} %collective-permute-done.1.refs_2_), channel_id=1, source_target_pairs={{0,1},{1,0},{2,3},{3,2},{4,5},{5,4},{6,7},{7,6},{8,9},{9,8},{10,11... | collective-permute-start | bytes 393224 | tf_op jit(solution)/shard_map/ppermute | solution.py:254
  13.0 3.4 %copy-start.7 = (bf16[256,16384]{1,0:T(8,128)(2,1)S(1)}, bf16[256,16384]{1,0:T(8,128)(2,1)}, u32[]{:S(2)}) copy-start(bf16[256,16384]{1,0:T(8,128)(2,1)} %refs_8_.1) | copy-start | bytes 25165828
  19.8 3.4 %copy-start.8 = (bf16[256,16384]{1,0:T(8,128)(2,1)S(1)}, bf16[256,16384]{1,0:T(8,128)(2,1)}, u32[]{:S(2)}) copy-start(bf16[256,16384]{1,0:T(8,128)(2,1)} %refs_8_.1) | copy-start | bytes 25165828
  37.2 11.1 %copy-start = (bf16[1024,16384]{1,0:T(8,128)(2,1)}, bf16[1024,16384]{1,0:T(8,128)(2,1)S(1)}, u32[]{:S(2)}) copy-start(bf16[1024,16384]{1,0:T(8,128)(2,1)S(1)} %get-tuple-element.34.e_ref) | copy-start | bytes 100663296
  48.2 4.3 %collective-permute-start.7 = (f32[128,128]{1,0:T(8,128)S(1)}, f32[128,128]{1,0:T(8,128)S(1)}, u32[]{:S(2)}, u32[]{:S(2)}) collective-permute-start(f32[128,128]{1,0:T(8,128)S(1)} %get-tuple-element.35), channel_id=1, source_target_pairs={{0,8},{8,0},{16,24},{24,16},{1,9},{9,1},{17,25},{25,17},{2,10},{10... | collective-permute-start | bytes 196616 | tf_op jit(solution)/shard_map/ppermute | solution.py:254
  52.5 5.2 %collective-permute-start.8 = (f32[128,128]{1,0:T(8,128)S(1)}, f32[128,128]{1,0:T(8,128)S(1)}, u32[]{:S(2)}, u32[]{:S(2)}) collective-permute-start(f32[128,128]{1,0:T(8,128)S(1)} %add.18.one_ref), channel_id=1, source_target_pairs={{0,16},{8,24},{16,0},{24,8},{1,17},{9,25},{17,1},{25,9},{2,18},{10... | collective-permute-start | bytes 196616 | tf_op jit(solution)/shard_map/ppermute | solution.py:254
  57.7 10.5 %copy-start.1 = (bf16[1024,16384]{1,0:T(8,128)(2,1)S(1)}, bf16[1024,16384]{1,0:T(8,128)(2,1)}, u32[]{:S(2)}) copy-start(bf16[1024,16384]{1,0:T(8,128)(2,1)} %copy-done) | copy-start | bytes 100663296
  75.5 2.5 %collective-permute-start.9 = (f32[8,128]{1,0:T(8,128)S(1)}, f32[8,128]{1,0:T(8,128)S(1)}, u32[]{:S(2)}, u32[]{:S(2)}) collective-permute-start(f32[8,128]{1,0:T(8,128)S(1)} %get-tuple-element.37), channel_id=1, source_target_pairs={{0,1},{1,0},{2,3},{3,2},{4,5},{5,4},{6,7},{7,6},{8,9},{9,8},{10,11... | collective-permute-start | bytes 12296 | tf_op jit(solution)/shard_map/ppermute | solution.py:254
  78.0 6.1 %collective-permute-start.12 = (f32[8,128]{1,0:T(8,128)S(1)}, f32[8,128]{1,0:T(8,128)S(1)}, u32[]{:S(2)}, u32[]{:S(2)}) collective-permute-start(f32[8,128]{1,0:T(8,128)S(1)} %add.19.refs_0_), channel_id=1, source_target_pairs={{0,6},{1,7},{2,4},{3,5},{4,2},{5,3},{6,0},{7,1},{8,14},{9,15},{10,... | collective-permute-start | bytes 12296 | tf_op jit(solution)/shard_map/ppermute | solution.py:254
  79.9 4.2 %collective-permute-start.11 = (f32[8,128]{1,0:T(8,128)S(1)}, f32[8,128]{1,0:T(8,128)S(1)}, u32[]{:S(2)}, u32[]{:S(2)}) collective-permute-start(f32[8,128]{1,0:T(8,128)S(1)} %add.19.refs_0_), channel_id=1, source_target_pairs={{0,4},{1,5},{2,6},{3,7},{4,0},{5,1},{6,2},{7,3},{8,12},{9,13},{10,... | collective-permute-start | bytes 12296 | tf_op jit(solution)/shard_map/ppermute | solution.py:254
  81.2 3.6 %collective-permute-start.10 = (f32[8,128]{1,0:T(8,128)S(1)}, f32[8,128]{1,0:T(8,128)S(1)}, u32[]{:S(2)}, u32[]{:S(2)}) collective-permute-start(f32[8,128]{1,0:T(8,128)S(1)} %add.19.refs_0_), channel_id=1, source_target_pairs={{0,2},{1,3},{2,0},{3,1},{4,6},{5,7},{6,4},{7,5},{8,10},{9,11},{10,... | collective-permute-start | bytes 12296 | tf_op jit(solution)/shard_map/ppermute | solution.py:254
  84.8 10.5 %copy-start.2 = (bf16[1024,16384]{1,0:T(8,128)(2,1)S(1)}, bf16[1024,16384]{1,0:T(8,128)(2,1)}, u32[]{:S(2)}) copy-start(bf16[1024,16384]{1,0:T(8,128)(2,1)} %copy-done) | copy-start | bytes 100663296
  100.3 4.3 %collective-permute-start.13 = (f32[128,128]{1,0:T(8,128)S(1)}, f32[128,128]{1,0:T(8,128)S(1)}, u32[]{:S(2)}, u32[]{:S(2)}) collective-permute-start(f32[128,128]{1,0:T(8,128)S(1)} %shard_map.53), channel_id=1, source_target_pairs={{0,8},{8,0},{16,24},{24,16},{1,9},{9,1},{17,25},{25,17},{2,10},{10... | collective-permute-start | bytes 196616 | tf_op jit(solution)/shard_map/ppermute | solution.py:254
  104.7 5.6 %collective-permute-start.14 = (f32[128,128]{1,0:T(8,128)S(1)}, f32[128,128]{1,0:T(8,128)S(1)}, u32[]{:S(2)}, u32[]{:S(2)}) collective-permute-start(f32[128,128]{1,0:T(8,128)S(1)} %add.20.one_ref), channel_id=1, source_target_pairs={{0,16},{8,24},{16,0},{24,8},{1,17},{9,25},{17,1},{25,9},{2,18},{10... | collective-permute-start | bytes 196616 | tf_op jit(solution)/shard_map/ppermute | solution.py:254
  110.3 10.5 %copy-start.3 = (bf16[1024,16384]{1,0:T(8,128)(2,1)S(1)}, bf16[1024,16384]{1,0:T(8,128)(2,1)}, u32[]{:S(2)}) copy-start(bf16[1024,16384]{1,0:T(8,128)(2,1)} %copy-done) | copy-start | bytes 100663296
  128.1 2.5 %collective-permute-start.15 = (f32[8,128]{1,0:T(8,128)S(1)}, f32[8,128]{1,0:T(8,128)S(1)}, u32[]{:S(2)}, u32[]{:S(2)}) collective-permute-start(f32[8,128]{1,0:T(8,128)S(1)} %get-tuple-element.39), channel_id=1, source_target_pairs={{0,1},{1,0},{2,3},{3,2},{4,5},{5,4},{6,7},{7,6},{8,9},{9,8},{10,11... | collective-permute-start | bytes 12296 | tf_op jit(solution)/shard_map/ppermute | solution.py:254
  130.6 6.1 %collective-permute-start.18 = (f32[8,128]{1,0:T(8,128)S(1)}, f32[8,128]{1,0:T(8,128)S(1)}, u32[]{:S(2)}, u32[]{:S(2)}) collective-permute-start(f32[8,128]{1,0:T(8,128)S(1)} %add.21.refs_0_), channel_id=1, source_target_pairs={{0,6},{1,7},{2,4},{3,5},{4,2},{5,3},{6,0},{7,1},{8,14},{9,15},{10,... | collective-permute-start | bytes 12296 | tf_op jit(solution)/shard_map/ppermute | solution.py:254
  132.2 4.6 %collective-permute-start.17 = (f32[8,128]{1,0:T(8,128)S(1)}, f32[8,128]{1,0:T(8,128)S(1)}, u32[]{:S(2)}, u32[]{:S(2)}) collective-permute-start(f32[8,128]{1,0:T(8,128)S(1)} %add.21.refs_0_), channel_id=1, source_target_pairs={{0,4},{1,5},{2,6},{3,7},{4,0},{5,1},{6,2},{7,3},{8,12},{9,13},{10,... | collective-permute-start | bytes 12296 | tf_op jit(solution)/shard_map/ppermute | solution.py:254
  133.1 3.6 %collective-permute-start.16 = (f32[8,128]{1,0:T(8,128)S(1)}, f32[8,128]{1,0:T(8,128)S(1)}, u32[]{:S(2)}, u32[]{:S(2)}) collective-permute-start(f32[8,128]{1,0:T(8,128)S(1)} %add.21.refs_0_), channel_id=1, source_target_pairs={{0,2},{1,3},{2,0},{3,1},{4,6},{5,7},{6,4},{7,5},{8,10},{9,11},{10,... | collective-permute-start | bytes 12296 | tf_op jit(solution)/shard_map/ppermute | solution.py:254
  136.7 10.5 %copy-start.4 = (bf16[1024,16384]{1,0:T(8,128)(2,1)S(1)}, bf16[1024,16384]{1,0:T(8,128)(2,1)}, u32[]{:S(2)}) copy-start(bf16[1024,16384]{1,0:T(8,128)(2,1)} %copy-done) | copy-start | bytes 100663296
  152.4 4.3 %collective-permute-start.19 = (f32[128,128]{1,0:T(8,128)S(1)}, f32[128,128]{1,0:T(8,128)S(1)}, u32[]{:S(2)}, u32[]{:S(2)}) collective-permute-start(f32[128,128]{1,0:T(8,128)S(1)} %shard_map.55), channel_id=1, source_target_pairs={{0,8},{8,0},{16,24},{24,16},{1,9},{9,1},{17,25},{25,17},{2,10},{10... | collective-permute-start | bytes 196616 | tf_op jit(solution)/shard_map/ppermute | solution.py:254
  156.7 5.6 %collective-permute-start.20 = (f32[128,128]{1,0:T(8,128)S(1)}, f32[128,128]{1,0:T(8,128)S(1)}, u32[]{:S(2)}, u32[]{:S(2)}) collective-permute-start(f32[128,128]{1,0:T(8,128)S(1)} %add.22.one_ref), channel_id=1, source_target_pairs={{0,16},{8,24},{16,0},{24,8},{1,17},{9,25},{17,1},{25,9},{2,18},{10... | collective-permute-start | bytes 196616 | tf_op jit(solution)/shard_map/ppermute | solution.py:254
  162.4 10.5 %copy-start.5 = (bf16[1024,16384]{1,0:T(8,128)(2,1)S(1)}, bf16[1024,16384]{1,0:T(8,128)(2,1)}, u32[]{:S(2)}) copy-start(bf16[1024,16384]{1,0:T(8,128)(2,1)} %copy-done) | copy-start | bytes 100663296
  180.4 10.5 %copy-start.6 = (bf16[1024,16384]{1,0:T(8,128)(2,1)S(1)}, bf16[1024,16384]{1,0:T(8,128)(2,1)}, u32[]{:S(2)}) copy-start(bf16[1024,16384]{1,0:T(8,128)(2,1)} %copy-done) | copy-start | bytes 100663296
  201.6 2.8 %collective-permute-start.21 = (f32[4,136,512]{2,1,0:T(8,128)S(1)}, f32[4,136,512]{2,1,0:T(8,128)S(1)}, u32[]{:S(2)}, u32[]{:S(2)}) collective-permute-start(f32[4,136,512]{2,1,0:T(8,128)S(1)} %get-tuple-element.61), channel_id=1, source_target_pairs={{0,1},{1,0},{2,3},{3,2},{4,5},{5,4},{6,7},{7,6},{8,9},{9,8},{10,11... | collective-permute-start | bytes 3342344 | tf_op jit(solution)/shard_map/ppermute | solution.py:254
  204.7 15.7 %copy-start.9 = (bf16[128,256]{1,0:T(8,128)(2,1)S(1)}, bf16[128,256]{1,0:T(8,128)(2,1)}, u32[]{:S(2)}) copy-start(bf16[128,256]{1,0:T(8,128)(2,1)} %student_ref.1) | copy-start | bytes 196612
  204.8 10.5 %collective-permute-start.24 = (f32[136,512]{1,0:T(8,128)S(1)}, f32[136,512]{1,0:T(8,128)S(1)}, u32[]{:S(2)}, u32[]{:S(2)}) collective-permute-start(f32[136,512]{1,0:T(8,128)S(1)} %get-tuple-element.64), channel_id=1, source_target_pairs={{0,6},{1,7},{2,4},{3,5},{4,2},{5,3},{6,0},{7,1},{8,14},{9,15},{10,... | collective-permute-start | bytes 835592 | tf_op jit(solution)/shard_map/ppermute | solution.py:254
  206.3 14.1 %collective-permute-start.23 = (f32[136,512]{1,0:T(8,128)S(1)}, f32[136,512]{1,0:T(8,128)S(1)}, u32[]{:S(2)}, u32[]{:S(2)}) collective-permute-start(f32[136,512]{1,0:T(8,128)S(1)} %get-tuple-element.65), channel_id=1, source_target_pairs={{0,4},{1,5},{2,6},{3,7},{4,0},{5,1},{6,2},{7,3},{8,12},{9,13},{10,... | collective-permute-start | bytes 835592 | tf_op jit(solution)/shard_map/ppermute | solution.py:254
  207.4 13.0 %collective-permute-start.22 = (f32[136,512]{1,0:T(8,128)S(1)}, f32[136,512]{1,0:T(8,128)S(1)}, u32[]{:S(2)}, u32[]{:S(2)}) collective-permute-start(f32[136,512]{1,0:T(8,128)S(1)} %get-tuple-element.66), channel_id=1, source_target_pairs={{0,2},{1,3},{2,0},{3,1},{4,6},{5,7},{6,4},{7,5},{8,10},{9,11},{10,... | collective-permute-start | bytes 835592 | tf_op jit(solution)/shard_map/ppermute | solution.py:254
